TPU v7x, 128 devices: a whole 4x4x4 slice. The times are simulated.
128 devices in a mesh: shell: 8 (over x, z_hi), rank: 16 (over z_lo, y, core).
Axes of the slice: x: 4, y: 4, z: 4 (z_hi: 2, z_lo: 2; z = z_hi * 2 + z_lo), core: 2. Of those that a mesh axis runs over, the one named last changes fastest.
Arguments:
- coefs: float32 [16, 3, 65536], P(None, None, ('shell', 'rank')), may hold values from -3 to 3
- radii: float32 [65536], P(('shell', 'rank')), may hold values from 0.5 to 2
- pair_blocks: int32 [2, 1024], P(None, ('shell', 'rank')), may hold values from 0 to 63, as said below
- pair_count: int32 [128], P(('shell', 'rank')), may hold values from 1 to 8
Outputs:
- intensity: float32 [65536], P(('shell', 'rank'))
Inputs may be any that keep to these rules, and one draw needn't show every extreme that they name: pair_blocks[0] is below 32; pair_blocks[1] differs from pair_blocks[0] and is below 32 in slots of the last shell group.
All inputs are finite; a program needn't handle non-finite values.
Results may differ from a plain program's by a relative error of at most 0.0003.
Values sent between devices are 32-bit elements; how exact they have to be, the bound alone decides.
No kernel may reach another device: no remote copies, remote signals or barrier semaphores. Data moves between devices by JAX's collectives and lax.ppermute only.
A program may use at most 64 MiB of HBM per device.

v0:
```python
import jax
import jax.numpy as jnp
from jax import lax
from jax.sharding import PartitionSpec as P

NCOEF = 16
TIMES = 64
BLOCK = 256


def passed_along(value, axis, steps):
    count = lax.axis_size(axis)
    leading, last = (max(0, -steps), min(count, count - steps))
    return lax.ppermute(value, axis, [(source, source + steps) for source in range(leading, last)])


def cheb_table(ncoef, times):
    node = -1.0 + (2.0 * jnp.arange(times, dtype=jnp.float32) + 1.0) / times
    order = jnp.arange(ncoef, dtype=jnp.float32)
    return jnp.cos(order[None, :] * jnp.arccos(node)[:, None])


def evaluate(table, coefs):
    flat = coefs.reshape(coefs.shape[0], -1)
    values = jnp.dot(
        table, flat, precision=lax.Precision.HIGHEST, preferred_element_type=jnp.float32
    )
    return values.reshape(table.shape[0], coefs.shape[1], coefs.shape[2])


def pair_terms(first_pos, second_pos, first_rad, second_rad):
    diff_x = first_pos[:, 0, :, None] - second_pos[:, 0, None, :]
    diff_y = first_pos[:, 1, :, None] - second_pos[:, 1, None, :]
    diff_z = first_pos[:, 2, :, None] - second_pos[:, 2, None, :]
    gap = diff_x * diff_x + diff_y * diff_y + diff_z * diff_z
    summed = first_rad[:, None] + second_rad[None, :]
    reach = summed * summed
    weight = reach[None, :, :] / (reach[None, :, :] + gap)
    factor = 1.0 / (first_pos.shape[0] * first_pos.shape[2])
    return (jnp.sum(weight, axis=(0, 2)) * factor, jnp.sum(weight, axis=(0, 1)) * factor)


def body(coefs, radii, pair_blocks, pair_count):
    table = cheb_table(NCOEF, TIMES)
    own_pos = evaluate(table, coefs)
    shell_pos, shell_rad = (
        lax.all_gather(own_pos, "rank", axis=2, tiled=True),
        lax.all_gather(radii, "rank", axis=0, tiled=True),
    )
    next_pos, next_rad = passed_along((shell_pos, shell_rad), "shell", -1)
    span = shell_rad.shape[0]
    block_len = BLOCK
    all_pos = jnp.concatenate([shell_pos, next_pos], axis=2)
    all_rad = jnp.concatenate([shell_rad, next_rad], axis=0)

    def credit(slot, total):
        first = pair_blocks[0, slot] * block_len
        second = pair_blocks[1, slot] * block_len
        row, col = pair_terms(
            lax.dynamic_slice_in_dim(all_pos, first, block_len, 2),
            lax.dynamic_slice_in_dim(all_pos, second, block_len, 2),
            lax.dynamic_slice_in_dim(all_rad, first, block_len, 0),
            lax.dynamic_slice_in_dim(all_rad, second, block_len, 0),
        )
        total = lax.dynamic_update_slice_in_dim(
            total, lax.dynamic_slice_in_dim(total, first, block_len, 0) + row, first, 0
        )
        total = lax.dynamic_update_slice_in_dim(
            total, lax.dynamic_slice_in_dim(total, second, block_len, 0) + col, second, 0
        )
        return total

    credited = lax.fori_loop(0, pair_count[0], credit, jnp.zeros((2 * span,), jnp.float32))
    own_part = credited[:span]
    next_part = credited[span:]
    returned = passed_along(next_part, "shell", 1)
    return lax.psum_scatter(own_part + returned, "rank", scatter_dimension=0, tiled=True)


def solution(mesh):
    placed = (
        P(None, None, ("shell", "rank")),
        P(("shell", "rank")),
        P(None, ("shell", "rank")),
        P(("shell", "rank")),
    )
    return jax.shard_map(
        body, mesh=mesh, in_specs=placed, out_specs=P(("shell", "rank")), check_vma=False
    )
```

profile of v0, /device:TPU:4, one launch (start us, length us, event | category | flops | bytes accessed | tf_op | source)
XLA Modules:
  0.0 386.4 jit_solution(8358817740413730915)
XLA Ops:
  6.6 0.8 copy-done
  7.4 1.3 fusion.2
  8.8 45.0 %all-gather.3.cloned.1.call-done = f32[64,3,8192]{2,0,1:T(8,128)} async-done(((f32[64,3,512]{2,0,1:T(8,128)}), f32[64,3,8192]{2,0,1:T(8,128)}) %all-gather.3.cloned.1.call-update) | async-done | bytes 6291472 | tf_op jit(solution)/shard_map/all_gather | solution.py:47
  53.8 4.8 %collective-permute-start.1 = (f32[64,3,8192]{2,0,1:T(8,128)}, f32[64,3,8192]{2,0,1:T(8,128)}, u32[]{:S(2)}, u32[]{:S(2)}) collective-permute-start(f32[64,3,8192]{2,0,1:T(8,128)} %all-gather.3.cloned.1.call-done), channel_id=1, source_target_pairs={{16,0},{32,16},{48,32},{64,48},{80,64},{96,80},{112,96},{17,1},{33... | collective-permute-start | bytes 18874376 | tf_op jit(solution)/shard_map/ppermute | solution.py:14
  58.6 18.7 %all-gather = f32[16,1,512]{2,1,0:T(1,128)S(1)} all-gather(f32[1,1,512]{2,1,0:T(1,128)} %bitcast.44), channel_id=1, replica_groups=mesh['shell'=8,'rank'=16] {'rank'}, dimensions={0}, use_global_device_ids=true | all-gather | bytes 34816 | tf_op jit(solution)/shard_map/all_gather | solution.py:48
  77.3 3.9 %collective-permute-start = (f32[8192]{0:T(1024)S(1)}, f32[8192]{0:T(1024)S(1)}, u32[]{:S(2)}, u32[]{:S(2)}) collective-permute-start(f32[8192]{0:T(1024)S(1)} %bitcast.42), channel_id=1, source_target_pairs={{16,0},{32,16},{48,32},{64,48},{80,64},{96,80},{112,96},{17,1},{33... | collective-permute-start | bytes 98312 | tf_op jit(solution)/shard_map/ppermute | solution.py:14
  81.2 114.7 %collective-permute-done = f32[8192]{0:T(1024)S(1)} collective-permute-done((f32[8192]{0:T(1024)S(1)}, f32[8192]{0:T(1024)S(1)}, u32[]{:S(2)}, u32[]{:S(2)}) %collective-permute-start) | collective-permute-done | bytes 32800 | tf_op jit(solution)/shard_map/ppermute | solution.py:14
  196.0 10.4 %pad_maximum_fusion = f32[64,3,16384]{2,0,1:T(8,128)} fusion(f32[64,3,8192]{2,0,1:T(8,128)} %collective-permute-done.1, f32[64,3,8192]{2,0,1:T(8,128)} %all-gather.3.cloned.1.call-done), kind=kLoop, calls=%fused_computation.14 | loop fusion | flops 3145728 | bytes 25165824 | tf_op jit(solution)/shard_map/concatenate | solution.py:53
  206.3 72.2 %while.10 = (s32[]{:T(128)}, f32[16384]{0:T(1024)S(1)}, s32[]{:T(128)}, s32[2,8]{1,0:T(2,128)S(1)}, f32[16384]{0:T(1024)S(1)}, /*index=5*/f32[64,3,16384]{2,0,1:...) while((s32[]{:T(128)}, f32[16384]{0:T(1024)S(1)}, ...), condition=%wide.region_3.0_spmd, body=%wide.region_0.0_spmd.sunk | while | flops 50463248 | bytes 1718599 | solution.py:73
  207.0 0.7 constant_dynamic-slice_fusion.3
  208.9 1.0 dynamic-slice_bitcast_fusion.7
  210.1 10.2 %fusion.17 = (f32[256]{0:T(256)S(1)}, f32[256]{0:T(256)S(1)}) fusion(f32[64,256]{1,0:T(8,128)S(1)} %get-tuple-element.133, f32[64,256]{1,0:T(8,128)S(1)} %get-tuple-element.134, f32[64,256]{1,0:T(8,128)S(1)} %get-tuple-element.135, f32[64,256]{1,0:T(8,128)S(1)} %get-tuple-element.136, f32[64,256]{1,0:T(8,128)S(1)} %get-tuple-element.137, ...), kind=kLoop, calls=%fused_computation.1.clone.1 | loop fusion | flops 50331136 | bytes 657408 | tf_op jit(solution)/shard_map/while/body/reduce_sum | solution.py:40
  220.3 0.2 add_dynamic-update-slice_fusion.4
  221.3 0.7 constant_dynamic-slice_fusion.3
  223.2 1.0 dynamic-slice_bitcast_fusion.7
  224.5 10.2 %fusion.17 = (f32[256]{0:T(256)S(1)}, f32[256]{0:T(256)S(1)}) fusion(f32[64,256]{1,0:T(8,128)S(1)} %get-tuple-element.133, f32[64,256]{1,0:T(8,128)S(1)} %get-tuple-element.134, f32[64,256]{1,0:T(8,128)S(1)} %get-tuple-element.135, f32[64,256]{1,0:T(8,128)S(1)} %get-tuple-element.136, f32[64,256]{1,0:T(8,128)S(1)} %get-tuple-element.137, ...), kind=kLoop, calls=%fused_computation.1.clone.1 | loop fusion | flops 50331136 | bytes 657408 | tf_op jit(solution)/shard_map/while/body/reduce_sum | solution.py:40
  235.6 0.7 constant_dynamic-slice_fusion.3
  237.5 1.0 dynamic-slice_bitcast_fusion.7
  238.8 10.2 %fusion.17 = (f32[256]{0:T(256)S(1)}, f32[256]{0:T(256)S(1)}) fusion(f32[64,256]{1,0:T(8,128)S(1)} %get-tuple-element.133, f32[64,256]{1,0:T(8,128)S(1)} %get-tuple-element.134, f32[64,256]{1,0:T(8,128)S(1)} %get-tuple-element.135, f32[64,256]{1,0:T(8,128)S(1)} %get-tuple-element.136, f32[64,256]{1,0:T(8,128)S(1)} %get-tuple-element.137, ...), kind=kLoop, calls=%fused_computation.1.clone.1 | loop fusion | flops 50331136 | bytes 657408 | tf_op jit(solution)/shard_map/while/body/reduce_sum | solution.py:40
  248.9 0.2 add_dynamic-update-slice_fusion.4
  249.9 0.7 constant_dynamic-slice_fusion.3
  251.8 1.0 dynamic-slice_bitcast_fusion.7
  253.1 10.2 %fusion.17 = (f32[256]{0:T(256)S(1)}, f32[256]{0:T(256)S(1)}) fusion(f32[64,256]{1,0:T(8,128)S(1)} %get-tuple-element.133, f32[64,256]{1,0:T(8,128)S(1)} %get-tuple-element.134, f32[64,256]{1,0:T(8,128)S(1)} %get-tuple-element.135, f32[64,256]{1,0:T(8,128)S(1)} %get-tuple-element.136, f32[64,256]{1,0:T(8,128)S(1)} %get-tuple-element.137, ...), kind=kLoop, calls=%fused_computation.1.clone.1 | loop fusion | flops 50331136 | bytes 657408 | tf_op jit(solution)/shard_map/while/body/reduce_sum | solution.py:40
  263.2 0.2 add_dynamic-update-slice_fusion.4
  264.3 0.7 constant_dynamic-slice_fusion.3
  266.2 1.0 dynamic-slice_bitcast_fusion.7
  267.4 10.2 %fusion.17 = (f32[256]{0:T(256)S(1)}, f32[256]{0:T(256)S(1)}) fusion(f32[64,256]{1,0:T(8,128)S(1)} %get-tuple-element.133, f32[64,256]{1,0:T(8,128)S(1)} %get-tuple-element.134, f32[64,256]{1,0:T(8,128)S(1)} %get-tuple-element.135, f32[64,256]{1,0:T(8,128)S(1)} %get-tuple-element.136, f32[64,256]{1,0:T(8,128)S(1)} %get-tuple-element.137, ...), kind=kLoop, calls=%fused_computation.1.clone.1 | loop fusion | flops 50331136 | bytes 657408 | tf_op jit(solution)/shard_map/while/body/reduce_sum | solution.py:40
  278.6 34.3 %collective-permute-start.2 = (f32[8192]{0:T(1024)S(1)}, f32[8192]{0:T(1024)S(1)}, u32[]{:S(2)}, u32[]{:S(2)}) collective-permute-start(f32[8192]{0:T(1024)S(1)} %slice.25), channel_id=1, source_target_pairs={{0,16},{16,32},{32,48},{48,64},{64,80},{80,96},{96,112},{1,17},{17... | collective-permute-start | bytes 98312 | tf_op jit(solution)/shard_map/ppermute | solution.py:14
  312.9 0.6 dynamic-slice
  314.2 0.3 collective-permute-done.2
  314.5 64.4 %all-reduce = f32[8192]{0:T(1024)S(1)} all-reduce(f32[8192]{0:T(1024)S(1)} %slice_add_fusion), channel_id=2, replica_groups=mesh['shell'=8,'rank'=16] {'rank'}, use_global_device_ids=true, to_apply=%region_4.0.clone | all-reduce | flops 8192 | bytes 65536
  378.9 0.7 dynamic-slice.1
  (30 shorter events, 2.2 us)
Async XLA Ops:
  6.5 0.9 copy-start
  6.5 47.2 %all-gather.3.cloned.1.call-start = ((), (), s32[]{:S(2)}) async-start(), calls=%async_computation | async-start | bytes 6684672 | tf_op jit(solution)/shard_map/all_gather | solution.py:47
  53.8 142.2 %collective-permute-start.1 = (f32[64,3,8192]{2,0,1:T(8,128)}, f32[64,3,8192]{2,0,1:T(8,128)}, u32[]{:S(2)}, u32[]{:S(2)}) collective-permute-start(f32[64,3,8192]{2,0,1:T(8,128)} %all-gather.3.cloned.1.call-done), channel_id=1, source_target_pairs={{16,0},{32,16},{48,32},{64,48},{80,64},{96,80},{112,96},{17,1},{33... | collective-permute-start | bytes 18874376 | tf_op jit(solution)/shard_map/ppermute | solution.py:14
  77.3 118.6 %collective-permute-start = (f32[8192]{0:T(1024)S(1)}, f32[8192]{0:T(1024)S(1)}, u32[]{:S(2)}, u32[]{:S(2)}) collective-permute-start(f32[8192]{0:T(1024)S(1)} %bitcast.42), channel_id=1, source_target_pairs={{16,0},{32,16},{48,32},{64,48},{80,64},{96,80},{112,96},{17,1},{33... | collective-permute-start | bytes 98312 | tf_op jit(solution)/shard_map/ppermute | solution.py:14
  195.9 10.4 %copy-start.1 = (s32[2,8]{1,0:T(2,128)S(1)}, s32[2,8]{1,0:T(2,128)}, u32[]{:S(2)}) copy-start(s32[2,8]{1,0:T(2,128)} %param.8) | copy-start | bytes 196
  195.9 117.0 %copy-start.2 = (u32[128]{0:T(128)S(1)}, u32[128]{0:T(128)}, u32[]{:S(2)}) copy-start(u32[128]{0:T(128)} %constant.34) | copy-start | bytes 1540
  278.6 35.9 %collective-permute-start.2 = (f32[8192]{0:T(1024)S(1)}, f32[8192]{0:T(1024)S(1)}, u32[]{:S(2)}, u32[]{:S(2)}) collective-permute-start(f32[8192]{0:T(1024)S(1)} %slice.25), channel_id=1, source_target_pairs={{0,16},{16,32},{32,48},{48,64},{64,80},{80,96},{96,112},{1,17},{17... | collective-permute-start | bytes 98312 | tf_op jit(solution)/shard_map/ppermute | solution.py:14
Sparse Core Ops, SparseCore 0:
  9.0 44.7 all-gather.2
where the time goes:
time: 392 us; the launch traced here: 386 us
  waiting for transfers between devices  160 us (41%)
  blocking collectives  83.1 us (21%)
  other arithmetic  63.5 us (16%)
  starting transfers between devices  43.1 us (11%)
  between operations  14.1 us (4%)
  local copies, waits for them, and re-layouts  11 us (3%)
  loops' own time  10.3 us (3%)
    ppermute x3, waiting for transfers between devices, passed_along(): lax.ppermute(value, axis, [(source, source + steps) for source in range(l...  115 us
    unnamed x1, blocking collectives  64.4 us
    reduce_sum x5, other arithmetic, pair_terms(): jnp.sum(weight, axis=(0, 1)) * factor  50.8 us
    all_gather x1, waiting for transfers between devices, body(): lax.all_gather(own_pos, 'rank', axis=2, tiled=True)  45 us
    ppermute x3, starting transfers between devices, passed_along(): lax.ppermute(value, axis, [(source, source + steps) for source in range(l...  43.1 us
    all_gather x1, blocking collectives, body(): lax.all_gather(radii, 'rank', axis=0, tiled=True)  18.7 us
    concatenate x1, other arithmetic, body(): all_pos = jnp.concatenate([shell_pos, next_pos], axis=2)  10.4 us
    another operation x1, loops' own time, body(): lax.fori_loop(0, pair_count[0], credit, jnp.zeros((2 * span,), jnp.float32))  10.3 us
  transfers between devices with their start and end apart: 4, of which 3 were waited for; matrix products, arithmetic and copies ran while one was open for 0% of the time, Pallas kernels for 0%

commit v1 on v0

v1 whole, which is shorter than its diff:
```python
import jax
import jax.numpy as jnp
import numpy as np
from jax import lax
from jax.experimental import pallas as pl
from jax.experimental.pallas import tpu as pltpu
from jax.sharding import PartitionSpec as P

NCOEF = 16
TIMES = 64
BLOCK = 256
RANKS = 16
SLOTS = 8
BLOCKS = 32
SPAN = BLOCKS * BLOCK
HELD = 512
UNROLL = 8
LIST = RANKS * SLOTS + UNROLL
TILE = 64
F32 = jnp.float32
BF16 = jnp.bfloat16
VMEM = pltpu.VMEM
SMEM = pltpu.SMEM
PARAMS = pltpu.CompilerParams(vmem_limit_bytes=56 * 1024 * 1024)


def passed_along(value, axis, steps):
    count = lax.axis_size(axis)
    leading, last = (max(0, -steps), min(count, count - steps))
    return lax.ppermute(value, axis, [(source, source + steps) for source in range(leading, last)])


def spread_table():
    node = -1.0 + (2.0 * np.arange(TIMES) + 1.0) / TIMES
    table = np.cos(np.arange(NCOEF)[None, :] * np.arccos(node)[:, None])
    spread = np.zeros((TIMES, 4, 3, NCOEF), np.float32)
    for c in range(3):
        spread[:, c, c, :] = table
    return spread.reshape(TIMES * 4, 3 * NCOEF)


def evaluate_kernel(pairs, count, table, coefs, radii, out):
    flat = jnp.concatenate([coefs[:, c, :] for c in range(3)], axis=0)
    values = jnp.dot(table[...], flat, precision=lax.Precision.HIGHEST, preferred_element_type=F32)
    lane = lax.broadcasted_iota(jnp.int32, (1, HELD), 1)
    info = jnp.where(lane == 2 * SLOTS, count[0].astype(F32), 0.0)
    for side in range(2):
        for slot in range(SLOTS):
            info = jnp.where(lane == side * SLOTS + slot, pairs[side, slot].astype(F32), info)
    row = lax.broadcasted_iota(jnp.int32, (16, HELD), 0)
    extra = jnp.where(row == 3, radii[...].reshape(1, HELD), jnp.where(row == 7, info, 0.0))
    out[...] = values.reshape(RANKS, 16, HELD) + extra[None]


def pieces(x):
    high = x.astype(BF16)
    rest = x - high.astype(F32)
    mid = rest.astype(BF16)
    low = (rest - mid.astype(F32)).astype(BF16)
    return high, mid, low


def features(slab):
    n = slab.shape[1]
    part = lax.broadcasted_iota(jnp.int32, (16, n), 0) % 4
    values = jnp.where(part == 3, jnp.broadcast_to(slab[3:4, :], (16, n)), slab)
    square = (values * values).reshape(2, 8, n)
    row = lax.broadcasted_iota(jnp.int32, (2, 8, n), 1)
    twos = square + jnp.where(row % 2 == 1, pltpu.roll(square, 1, 1), pltpu.roll(square, 7, 1))
    fours = twos + jnp.where((row // 2) % 2 == 1, pltpu.roll(twos, 2, 1), pltpu.roll(twos, 6, 1))
    high, mid, low = pieces(values)
    s_high, s_mid, s_low = (p.astype(F32) for p in pieces(fours.reshape(16, n)))
    zero = jnp.zeros((16, n), F32)
    sums = jnp.where(part == 0, s_high, jnp.where(part == 1, s_mid, jnp.where(part == 2, s_low, zero)))
    ones = jnp.where(part == 3, zero, 1.0)
    return high, mid, low, sums, ones, part


def prepare_second(second, second_radii, received, rank):
    slab = received[rank]
    high, mid, low, sums, ones, _ = features(slab)
    terms = (high, mid, high, low, high, mid, sums.astype(BF16), ones.astype(BF16))
    for i, term in enumerate(terms):
        second[16 * i : 16 * i + 16, rank * HELD : (rank + 1) * HELD] = term
    for half in range(HELD // BLOCK):
        block = rank * (HELD // BLOCK) + half
        second_radii[block : block + 1, :] = slab[3:4, half * BLOCK : (half + 1) * BLOCK]


def prepare_first(first, first_radii, received, rank):
    slab = received[rank]
    high, mid, low, sums, ones, part = features(slab)
    scale = jnp.where(part == 3, 2.0, -2.0)
    high, mid, low = (scale * p.astype(F32) for p in (high, mid, low))
    terms = jnp.concatenate([high, high, mid, high, low, mid, ones, sums], axis=0)
    for c in range(0, HELD, 128):
        at = rank * HELD + c
        first[at : at + 128, :] = terms[:, c : c + 128].T.astype(BF16)
        first_radii[at : at + 128, :] = jnp.broadcast_to(slab[3:4, c : c + 128], (128, 128)).T


def credit_pair(first, first_radii, second, second_radii, rows, columns, a, b):
    from_a = pl.multiple_of(lax.rem(a, BLOCKS) * BLOCK, BLOCK)
    block_b = lax.rem(b, BLOCKS)
    of_b = second[:, pl.ds(pl.multiple_of(block_b * BLOCK, BLOCK), BLOCK)]
    radii_b = second_radii[pl.ds(block_b, 1), :]
    lane = lax.broadcasted_iota(jnp.int32, (TILE, 128), 1)
    masks = [jnp.where((lane % 16) // 4 == t, 1.0, 0.0).astype(BF16) for t in range(4)]
    column = jnp.zeros((8, BLOCK), F32)
    for i in range(0, BLOCK, TILE):
        of_a = first[pl.ds(from_a + i, TILE), :]
        total = None
        for mask in masks:
            whole = jnp.dot(of_a * mask, of_b, preferred_element_type=F32)
            inverse = pl.reciprocal(whole, approx=False)
            total = inverse if total is None else total + inverse
        radii_a = first_radii[pl.ds(from_a + i, TILE), :]
        summed = jnp.concatenate([radii_a, radii_a], axis=1) + radii_b
        weight = total * (summed * summed)
        column = column + jnp.sum(weight.reshape(TILE // 8, 8, BLOCK), axis=0)
        row = jnp.sum(weight[:, :128] + weight[:, 128:], axis=1, keepdims=True)
        rows[i : i + TILE, :] = rows[i : i + TILE, :] + jnp.where(lane == a, row, 0.0)
    at = pl.ds(pl.multiple_of(b * 8, 8), 8)
    columns[at, :] = columns[at, :] + column


def credit_list(first, first_radii, second, second_radii, rows, columns, pairs, count):
    rows[...] = jnp.zeros_like(rows)
    columns[...] = jnp.zeros_like(columns)

    @pl.loop(0, (count + UNROLL - 1) // UNROLL)
    def _(step):
        for u in range(UNROLL):
            at = step * UNROLL + u
            credit_pair(first, first_radii, second, second_radii, rows, columns, pairs[0, at], pairs[1, at])


def block_sums(columns):
    return jnp.sum(columns[0 : 8 * BLOCKS, :].reshape(BLOCKS, 8, BLOCK), axis=1)


def own_kernel(
    received, credited, first, first_radii, crossing,
    second, second_radii, rows, columns, info, lists, own, sem,
):
    info[...] = received[:, 7, 0:128].astype(jnp.int32)
    copy = pltpu.make_async_copy(info, lists, sem)
    copy.start()
    for rank in range(RANKS):
        prepare_second(second, second_radii, received, rank)
        prepare_first(first, first_radii, received, rank)
    copy.wait()

    def gather(device, counts):
        def slot(k, counts):
            a, b = lists[device, k], lists[device, SLOTS + k]
            n_own, n_cross = counts
            crosses = b >= BLOCKS
            own[0, n_own] = a
            own[1, n_own] = b
            crossing[0, n_cross] = a
            crossing[1, n_cross] = b - BLOCKS
            return (n_own + jnp.where(crosses, 0, 1), n_cross + jnp.where(crosses, 1, 0))

        return lax.fori_loop(0, lists[device, 2 * SLOTS], slot, counts)

    n_own, n_cross = lax.fori_loop(0, RANKS, gather, (jnp.int32(0), jnp.int32(0)))
    for u in range(UNROLL):
        for side in range(2):
            own[side, n_own + u] = BLOCKS
            crossing[side, n_cross + u] = BLOCKS
    crossing[2, 0] = n_cross
    credit_list(first, first_radii, second, second_radii, rows, columns, own, n_own)
    credited[...] = rows[...].T[0:BLOCKS, :] + block_sums(columns)


def cross_kernel(
    crossing, received, earlier, first_hbm, first_radii_hbm, out,
    first, first_radii, second, second_radii, rows, columns, sem,
):
    copies = [
        pltpu.make_async_copy(first_hbm, first, sem.at[0]),
        pltpu.make_async_copy(first_radii_hbm, first_radii, sem.at[1]),
    ]
    for copy in copies:
        copy.start()
    for rank in range(RANKS):
        prepare_second(second, second_radii, received, rank)
    for copy in copies:
        copy.wait()
    credit_list(first, first_radii, second, second_radii, rows, columns, crossing, crossing[2, 0])
    factor = 1.0 / (TIMES * BLOCK)
    own = (earlier[...] + rows[...].T[0:BLOCKS, :]) * factor
    beyond = block_sums(columns) * factor
    for block in range(BLOCKS):
        rank, half = divmod(block, 2)
        for k in range(2):
            at = 2 * half + k
            out[rank, at : at + 1, :] = own[block : block + 1, k * 128 : (k + 1) * 128]
            out[rank, 4 + at : 5 + at, :] = beyond[block : block + 1, k * 128 : (k + 1) * 128]


def body(coefs, radii, pair_blocks, pair_count):
    in_vmem, in_smem = pl.BlockSpec(memory_space=VMEM), pl.BlockSpec(memory_space=SMEM)
    anywhere = pl.BlockSpec(memory_space=pl.ANY)
    at_all = pl.pallas_call(
        evaluate_kernel,
        out_shape=jax.ShapeDtypeStruct((RANKS, 16, HELD), F32),
        in_specs=[in_smem, in_smem, in_vmem, in_vmem, in_vmem],
        out_specs=in_vmem,
        compiler_params=PARAMS,
        name="evaluate",
    )(pair_blocks, pair_count, jnp.asarray(spread_table()), coefs, radii)
    received = lax.all_to_all(at_all, "rank", 0, 0)
    beyond = passed_along(received, "shell", -1)
    credited, first, first_radii, crossing = pl.pallas_call(
        own_kernel,
        out_shape=[
            jax.ShapeDtypeStruct((BLOCKS, BLOCK), F32),
            jax.ShapeDtypeStruct((SPAN, 128), BF16),
            jax.ShapeDtypeStruct((SPAN, 128), F32),
            jax.ShapeDtypeStruct((3, LIST), jnp.int32),
        ],
        in_specs=[in_vmem],
        out_specs=[in_vmem, in_vmem, in_vmem, in_smem],
        scratch_shapes=[
            VMEM((128, SPAN), BF16),
            VMEM((BLOCKS, BLOCK), F32),
            VMEM((BLOCK, 128), F32),
            VMEM((8 * BLOCKS + 8, BLOCK), F32),
            VMEM((RANKS, 128), jnp.int32),
            SMEM((RANKS, 128), jnp.int32),
            SMEM((2, LIST), jnp.int32),
            pltpu.SemaphoreType.DMA,
        ],
        compiler_params=PARAMS,
        cost_estimate=pl.CostEstimate(flops=8_000_000_000, bytes_accessed=8_000_000, transcendentals=0),
        name="own_pairs",
    )(received)
    partial = pl.pallas_call(
        cross_kernel,
        out_shape=jax.ShapeDtypeStruct((RANKS, 8, 128), F32),
        in_specs=[in_smem, in_vmem, in_vmem, anywhere, anywhere],
        out_specs=in_vmem,
        scratch_shapes=[
            VMEM((SPAN, 128), BF16),
            VMEM((SPAN, 128), F32),
            VMEM((128, SPAN), BF16),
            VMEM((BLOCKS, BLOCK), F32),
            VMEM((BLOCK, 128), F32),
            VMEM((8 * BLOCKS + 8, BLOCK), F32),
            pltpu.SemaphoreType.DMA((2,)),
        ],
        compiler_params=PARAMS,
        cost_estimate=pl.CostEstimate(flops=8_000_000_000, bytes_accessed=8_000_000, transcendentals=0),
        name="crossing_pairs",
    )(crossing, beyond, credited, first, first_radii)
    summed = jnp.sum(lax.all_to_all(partial, "rank", 0, 0), axis=0)
    returned = passed_along(summed[4:], "shell", 1)
    return (summed[:4] + returned).reshape(HELD)


def solution(mesh):
    placed = (
        P(None, None, ("shell", "rank")),
        P(("shell", "rank")),
        P(None, ("shell", "rank")),
        P(("shell", "rank")),
    )
    return jax.shard_map(
        body, mesh=mesh, in_specs=placed, out_specs=P(("shell", "rank")), check_vma=False
    )
```

time: 392 us -> 73.3 us (0.19); the launches traced: 386 us -> 73.7 us
  waiting for transfers between devices: 160 us -> 4.46 us
  other arithmetic: 63.5 us -> 0.6 us
  blocking collectives: 83.1 us -> 26.3 us
  starting transfers between devices: 43.1 us -> 8.87 us
  Pallas kernels: 0 us -> 30.3 us
  between operations: 14.1 us -> 0.71 us
  loops' own time: 10.3 us -> 0 us
  local copies, waits for them, and re-layouts: 11 us -> 2.41 us
    ppermute x3 -> x2, waiting for transfers between devices: 115 us -> 4.46 us  [passed_along(): lax.ppermute(value, axis, [(source, source + steps) for source in range(l...]
    unnamed x1 -> x0, blocking collectives: 64.4 us -> none
    reduce_sum x5 -> x1, other arithmetic: 50.8 us -> 0.02 us  [body(): summed = jnp.sum(lax.all_to_all(partial, 'rank', 0, 0), axis=0)]
    all_gather x1 -> x0, waiting for transfers between devices: 45 us -> none  [body(): lax.all_gather(own_pos, 'rank', axis=2, tiled=True)]
    ppermute x3 -> x2, starting transfers between devices: 43.1 us -> 8.87 us  [passed_along(): lax.ppermute(value, axis, [(source, source + steps) for source in range(l...]
    pallas_call x0 -> x3, Pallas kernels: none -> 30.3 us  [the longest x1 14.9 us: body(): pl.pallas_call(own_kernel, out_shape=[jax.ShapeDtypeStruct((BLOCKS, BLOCK...]
    all_to_all x0 -> x2, blocking collectives: none -> 26.3 us  [the longest x1 16.8 us: body(): received = lax.all_to_all(at_all, 'rank', 0, 0)]
    all_gather x1 -> x0, blocking collectives: 18.7 us -> none  [body(): lax.all_gather(radii, 'rank', axis=0, tiled=True)]
  transfers between devices with their start and end apart: 4 -> 2, of which waited for: 3 -> 1; matrix products, arithmetic and copies ran while one was open for 0% -> 0% of each run, Pallas kernels for 0% -> 20%
where the time goes in v1:
time: 73.3 us; the launch traced here: 73.7 us
  Pallas kernels  30.3 us (41%)
  blocking collectives  26.3 us (36%)
  starting transfers between devices  8.87 us (12%)
  waiting for transfers between devices  4.46 us (6%)
  local copies, waits for them, and re-layouts  2.41 us (3%)
    all_to_all x1, blocking collectives, body(): received = lax.all_to_all(at_all, 'rank', 0, 0)  16.8 us
    pallas_call x1, Pallas kernels, body(): pl.pallas_call(own_kernel, out_shape=[jax.ShapeDtypeStruct((BLOCKS, BLOCK...  14.9 us
    pallas_call x1, Pallas kernels, body(): pl.pallas_call(cross_kernel, out_shape=jax.ShapeDtypeStruct((RANKS, 8, 12...  13 us
    all_to_all x1, blocking collectives, body(): summed = jnp.sum(lax.all_to_all(partial, 'rank', 0, 0), axis=0)  9.57 us
    ppermute x2, starting transfers between devices, passed_along(): lax.ppermute(value, axis, [(source, source + steps) for source in range(l...  8.87 us
    ppermute x2, waiting for transfers between devices, passed_along(): lax.ppermute(value, axis, [(source, source + steps) for source in range(l...  4.46 us
    unnamed x5, local copies, waits for them, and re-layouts  2.41 us
    pallas_call x1, Pallas kernels, body(): pl.pallas_call(evaluate_kernel, out_shape=jax.ShapeDtypeStruct((RANKS, 16...  2.35 us
  transfers between devices with their start and end apart: 2, of which 1 were waited for; matrix products, arithmetic and copies ran while one was open for 0% of the time, Pallas kernels for 20%

profile of v1, /device:TPU:4, one launch (start us, length us, event | category | flops | bytes accessed | tf_op | source)
XLA Modules:
  0.0 73.7 jit_solution(5450032548806331183)
XLA Ops:
  0.7 1.6 %copy.6.coefs = f32[16,3,512]{2,1,0:T(4,128)} copy(f32[16,3,512]{2,0,1:T(8,128)} %param.5) | data formatting | bytes 196608 | tf_op args[0]
  2.3 2.3 %evaluate.1 = f32[16,16,512]{2,1,0:T(8,128)} custom-call(s32[2,8]{1,0:T(2,128)} %pairs.1, s32[1]{0:T(128)S(6)} %copy.7.count, f32[256,48]{1,0:T(8,128)} %constant.4.clone.table, f32[16,3,512]{2,1,0:T(4,128)} %copy.6.coefs, f32[512]{0:T(512)} %radii.1), custom_call_target="tpu_custom_call" | custom-call | tf_op jit(solution)/shard_map/evaluate/pallas_call | solution.py:206
  4.6 16.8 %all_to_all.10.received = f32[16,16,512]{2,1,0:T(8,128)S(1)} all-to-all(f32[16,16,512]{2,1,0:T(8,128)} %evaluate.1), channel_id=1, replica_groups=mesh['shell'=8,'rank'=16] {'rank'}, dimensions={0} | all-to-all | bytes 1048576 | tf_op jit(solution)/shard_map/all_to_all | solution.py:214
  21.4 0.0 copy-start
  21.4 5.4 %collective-permute-start = (f32[16,16,512]{2,1,0:T(8,128)S(1)}, f32[16,16,512]{2,1,0:T(8,128)S(1)}, u32[]{:S(2)}, u32[]{:S(2)}) collective-permute-start(f32[16,16,512]{2,1,0:T(8,128)S(1)} %all_to_all.10.received), channel_id=1, source_target_pairs={{16,0},{32,16},{48,32},{64,48},{80,64},{96,80},{112,96},{17,1},{33... | collective-permute-start | bytes 1572872 | tf_op jit(solution)/shard_map/ppermute | solution.py:30
  26.9 0.0 copy-done
  26.9 14.9 %own_pairs.1 = (f32[32,256]{1,0:T(8,128)}, bf16[8192,128]{1,0:T(8,128)(2,1)}, f32[8192,128]{1,0:T(8,128)}, s32[3,136]{1,0:T(4,128)}) custom-call(f32[16,16,512]{2,1,0:T(8,128)} %copy-done), custom_call_target="tpu_custom_call" | custom-call | flops 8000000000 | bytes 8000000 | tf_op jit(solution)/shard_map/own_pairs/pallas_call | solution.py:216
  41.7 0.0 collective-permute-done.received
  41.8 0.0 copy-start.1
  41.8 0.8 %copy-done.1 = f32[16,16,512]{2,1,0:T(8,128)} copy-done((f32[16,16,512]{2,1,0:T(8,128)}, f32[16,16,512]{2,1,0:T(8,128)S(1)}, u32[]{:S(2)}) %copy-start.1) | copy-done | bytes 524312
  42.6 13.0 %crossing_pairs.1 = f32[16,8,128]{2,1,0:T(8,128)} custom-call(s32[3,136]{1,0:T(4,128)} %get-tuple-element.9.crossing, f32[16,16,512]{2,1,0:T(8,128)} %copy-done.1, f32[32,256]{1,0:T(8,128)} %get-tuple-element.10.earlier, bf16[8192,128]{1,0:T(8,128)(2,1)} %get-tuple-element.11.first_hbm, f32[8192,128]{1,0:T(8,128)} %get-tuple-element.12.first_radii_hbm), custom_call_target="tpu_custom_call" | custom-call | flops 8000000000 | bytes 8000000 | tf_op jit(solution)/shard_map/crossing_pairs/pallas_call | solution.py:240
  55.6 9.6 %all_to_all.11 = f32[16,8,128]{2,1,0:T(8,128)S(1)} all-to-all(f32[16,8,128]{2,1,0:T(8,128)} %crossing_pairs.1), channel_id=1, replica_groups=mesh['shell'=8,'rank'=16] {'rank'}, dimensions={0} | all-to-all | bytes 131072 | tf_op jit(solution)/shard_map/all_to_all | solution.py:258
  65.2 3.4 %collective-permute-start.1 = (f32[4,128]{1,0:T(4,128)S(1)}, f32[4,128]{1,0:T(4,128)S(1)}, u32[]{:S(2)}, u32[]{:S(2)}) collective-permute-start(f32[4,128]{1,0:T(4,128)S(1)} %slice.7), channel_id=1, source_target_pairs={{0,16},{16,32},{32,48},{48,64},{64,80},{80,96},{96,112},{1,17},{17... | collective-permute-start | bytes 6152 | tf_op jit(solution)/shard_map/ppermute | solution.py:30
  68.6 4.5 %collective-permute-done.1 = f32[4,128]{1,0:T(4,128)S(1)} collective-permute-done((f32[4,128]{1,0:T(4,128)S(1)}, f32[4,128]{1,0:T(4,128)S(1)}, u32[]{:S(2)}, u32[]{:S(2)}) %collective-permute-start.1) | collective-permute-done | bytes 2080 | tf_op jit(solution)/shard_map/ppermute | solution.py:30
  73.1 0.6 add_bitcast_fusion
  (2 shorter events, 0.0 us)
Async XLA Ops:
  21.4 5.5 %copy-start = (f32[16,16,512]{2,1,0:T(8,128)}, f32[16,16,512]{2,1,0:T(8,128)S(1)}, u32[]{:S(2)}) copy-start(f32[16,16,512]{2,1,0:T(8,128)S(1)} %all_to_all.10.received) | copy-start | bytes 1572868
  21.4 20.4 %collective-permute-start = (f32[16,16,512]{2,1,0:T(8,128)S(1)}, f32[16,16,512]{2,1,0:T(8,128)S(1)}, u32[]{:S(2)}, u32[]{:S(2)}) collective-permute-start(f32[16,16,512]{2,1,0:T(8,128)S(1)} %all_to_all.10.received), channel_id=1, source_target_pairs={{16,0},{32,16},{48,32},{64,48},{80,64},{96,80},{112,96},{17,1},{33... | collective-permute-start | bytes 1572872 | tf_op jit(solution)/shard_map/ppermute | solution.py:30
  41.8 0.8 %copy-start.1 = (f32[16,16,512]{2,1,0:T(8,128)}, f32[16,16,512]{2,1,0:T(8,128)S(1)}, u32[]{:S(2)}) copy-start(f32[16,16,512]{2,1,0:T(8,128)S(1)} %collective-permute-done.received) | copy-start | bytes 1572868
  65.2 7.9 %collective-permute-start.1 = (f32[4,128]{1,0:T(4,128)S(1)}, f32[4,128]{1,0:T(4,128)S(1)}, u32[]{:S(2)}, u32[]{:S(2)}) collective-permute-start(f32[4,128]{1,0:T(4,128)S(1)} %slice.7), channel_id=1, source_target_pairs={{0,16},{16,32},{32,48},{48,64},{64,80},{80,96},{96,112},{1,17},{17... | collective-permute-start | bytes 6152 | tf_op jit(solution)/shard_map/ppermute | solution.py:30
